TPU v7x, 32 devices: a whole 2x2x4 slice. The times are simulated.
32 devices in a mesh: row: 8 (over z, y), col: 4 (over x, core).
Axes of the slice: x: 2, y: 2, z: 4, core: 2. Of those that a mesh axis runs over, the one named last changes fastest.
Arguments:
- amplitudes: bfloat16 [4096, 16384], P(('row', 'col')), may hold values from -6 to 6
- amp_tiles: int32 [64, 256], P(('row', 'col')), may hold values 0 or 1
- integrals: bfloat16 [512, 16384], P('row', 'col'), may hold values from -0.046875 to 0.046875
- int_tiles: int32 [8, 256], P(None, 'col'), may hold values 0 or 1
Outputs:
- ladder: bfloat16 [512, 4096], P('col', 'row')
All inputs are finite; a program needn't handle non-finite values. No bound on the sum of `amp_tiles` or of `int_tiles` on one device may be relied on, other than what follows from the above.
Results may differ from a plain program's by a relative error of at most 0.001.
Values may be sent and summed in bfloat16 or wider, within the bound.
A program may use at most 64 MiB of HBM per device.

v0:
```python
import jax
import jax.numpy as jnp
from jax import lax
from jax.sharding import PartitionSpec as P

TILE = 64


def expand_mask(tiles):
    return jnp.repeat(jnp.repeat(tiles, TILE, axis=0), TILE, axis=1).astype(jnp.bfloat16)


def local(amplitudes, amp_tiles, integrals, int_tiles):
    regrouped, regrouped_tiles = (
        lax.all_to_all(amplitudes, "col", split_axis=1, concat_axis=0, tiled=True),
        lax.all_to_all(amp_tiles, "col", split_axis=1, concat_axis=0, tiled=True),
    )
    stored_amps = regrouped * expand_mask(regrouped_tiles)
    panel_mask = expand_mask(int_tiles)
    partial_sums = lax.dot_general(
        lax.all_gather(integrals, "row", axis=0, tiled=True) * panel_mask,
        stored_amps,
        (((1,), (1,)), ((), ())),
        preferred_element_type=jnp.float32,
    )
    summed = lax.psum_scatter(partial_sums, "col", scatter_dimension=0, tiled=True)
    return summed.astype(jnp.bfloat16)


def solution(mesh):
    return jax.shard_map(
        local,
        mesh=mesh,
        in_specs=(
            P(("row", "col"), None),
            P(("row", "col"), None),
            P("row", "col"),
            P(None, "col"),
        ),
        out_specs=P("col", "row"),
        check_vma=False,
    )
```

profile of v0, /device:TPU:0, one launch (start us, length us, event | category | flops | bytes accessed | tf_op | source)
XLA Modules:
  0.0 132.4 jit_solution(1341471302888487965)
XLA Ops:
  6.5 0.0 all-gather.2.cloned.1.call-start
  6.5 0.7 all-gather.2.cloned.1.call-update
  7.3 0.8 all_to_all.28
  8.0 0.7 reshape.15
  8.7 4.2 %all-to-all-start.1 = ((s32[4,1,128]{2,1,0:T(1,128)}), s32[4,1,128]{2,1,0:T(1,128)S(1)}, u32[]{:S(2)}, u32[]{:S(2)}) async-start(s32[4,1,128]{2,1,0:T(1,128)} %reshape.15), calls=%async_computation.1 | async-start | bytes 4096 | tf_op jit(solution)/shard_map/all_to_all | solution.py:16
  12.9 6.4 %copy.19 = bf16[128,16384]{0,1:T(8,128)(2,1)} copy(bf16[128,16384]{1,0:T(8,128)(2,1)} %param.4) | data formatting | bytes 8388608 | tf_op args[0]
  19.3 0.0 all-to-all-done.1
  19.3 0.0 copy-start.1
  19.3 5.0 %all-to-all-start = ((bf16[128,4,4096]{0,2,1:T(8,128)(2,1)}), bf16[128,4,4096]{0,2,1:T(8,128)(2,1)}, u32[]{:S(2)}, u32[]{:S(2)}) async-start(bf16[128,4,4096]{0,2,1:T(8,128)(2,1)} %bitcast.21), calls=%async_computation | async-start | bytes 8388608 | tf_op jit(solution)/shard_map/all_to_all | solution.py:15
  24.3 0.0 reduce-scatter.2.cloned.1.call-start
  24.3 0.0 copy-done.1
  24.3 0.1 copy.17
  24.4 0.1 broadcast_in_dim.12
  24.6 0.1 convert_element_type.32
  24.7 0.5 broadcast.4
  25.2 0.7 reduce
  25.9 0.1 reshape.16
  26.0 0.1 copy.22
  26.1 0.1 broadcast_in_dim.14
  26.2 0.1 convert_element_type.37
  26.4 2.3 %broadcast_in_dim.15 = bf16[512,64,64]{0,2,1:T(8,128)(2,1)} broadcast(bf16[512,64]{0,1:T(8,128)(2,1)S(1)} %convert_element_type.37), dimensions={0,1} | broadcast | bytes 4259840 | tf_op jit(solution)/shard_map/broadcast_in_dim | solution.py:10
  28.6 6.4 %copy.23 = bf16[512,4096]{1,0:T(8,128)(2,1)} copy(bf16[512,4096]{0,1:T(8,128)(2,1)} %bitcast.22) | data formatting | bytes 8388608 | tf_op jit(solution)/shard_map/convert_element_type | solution.py:10
  35.0 37.5 %all-to-all-done = bf16[128,4,4096]{0,2,1:T(8,128)(2,1)} async-done(((bf16[128,4,4096]{0,2,1:T(8,128)(2,1)}), bf16[128,4,4096]{0,2,1:T(8,128)(2,1)}, u32[]{:S(2)}, u32[]{:S(2)}) %all-to-all-start) | async-done | bytes 4194336 | tf_op jit(solution)/shard_map/all_to_all | solution.py:15
  72.5 6.4 %copy.20 = bf16[4,128,4096]{2,1,0:T(8,128)(2,1)} copy(bf16[4,128,4096]{1,2,0:T(8,128)(2,1)} %bitcast.2) | data formatting | bytes 8388608 | tf_op jit(solution)/shard_map/all_to_all | solution.py:15
  79.0 5.9 %bitcast_multiply_fusion = bf16[512,4096]{1,0:T(8,128)(2,1)} fusion(bf16[512,4096]{1,0:T(8,128)(2,1)} %copy.23, bf16[4,128,4096]{2,1,0:T(8,128)(2,1)} %copy.20), kind=kLoop, calls=%fused_computation | loop fusion | flops 2097152 | bytes 12582912 | tf_op jit(solution)/shard_map/mul | solution.py:18
  84.8 0.8 all-gather.2.cloned.1.call-done
  85.6 6.5 %copy.18 = bf16[512,4096]{0,1:T(8,128)(2,1)} copy(bf16[512,4096]{1,0:T(8,128)(2,1)} %all-gather.2.cloned.1.call-done) | data formatting | bytes 8388608 | tf_op jit(solution)/shard_map/all_gather | solution.py:21
  92.1 0.0 copy-start
  92.1 2.6 %bitcast_multiply_fusion.1 = bf16[512,4096]{0,1:T(8,128)(2,1)S(1)} fusion(bf16[512,4096]{0,1:T(8,128)(2,1)} %copy.18, bf16[512,64]{0,1:T(8,128)(2,1)S(1)} %convert_element_type.32), kind=kLoop, calls=%fused_computation.1 | loop fusion | flops 2097152 | bytes 8454144 | tf_op jit(solution)/shard_map/mul | solution.py:21
  94.7 0.8 copy-done
  95.6 3.3 %fusion = f32[512,512]{1,0:T(8,128)} fusion(bf16[512,4096]{0,1:T(8,128)(2,1)S(1)} %bitcast_multiply_fusion.1, bf16[512,4096]{1,0:T(8,128)(2,1)S(1)} %copy-done), kind=kOutput, calls=%fused_computation.4 | convolution fusion | flops 2147483648 | bytes 9437184 | tf_op jit(solution)/shard_map/dot_general | solution.py:20
  98.9 0.0 reduce-scatter.2.cloned.1.call-update
  98.9 25.0 %reduce-scatter.2.cloned.1.call-done = f32[128,512]{1,0:T(8,128)} async-done(((f32[512,512]{1,0:T(8,128)}), f32[128,512]{1,0:T(8,128)}) %reduce-scatter.2.cloned.1.call-update) | async-done | bytes 262160 | tf_op jit(solution)/shard_map/reduce_scatter | solution.py:26
  123.9 1.6 %convert_element_type.39 = bf16[128,512]{1,0:T(8,128)(2,1)} convert(f32[128,512]{1,0:T(8,128)} %reduce-scatter.2.cloned.1.call-done) | non-fusion elementwise | flops 65536 | bytes 393216 | tf_op jit(solution)/shard_map/convert_element_type | solution.py:27
  (3 shorter events, 0.0 us)
Async XLA Ops:
  6.5 79.1 %all-gather.2.cloned.1.call-start = ((), (), s32[]{:S(2)}) async-start(), calls=%async_computation.3 | async-start | bytes 4718592 | tf_op jit(solution)/shard_map/all_gather | solution.py:21
  8.7 10.6 %all-to-all-start.1 = ((s32[4,1,128]{2,1,0:T(1,128)}), s32[4,1,128]{2,1,0:T(1,128)S(1)}, u32[]{:S(2)}, u32[]{:S(2)}) async-start(s32[4,1,128]{2,1,0:T(1,128)} %reshape.15), calls=%async_computation.1 | async-start | bytes 4096 | tf_op jit(solution)/shard_map/all_to_all | solution.py:16
  19.3 5.0 %copy-start.1 = (s32[8,64]{1,0:T(8,128)S(1)}, s32[8,64]{1,0:T(8,128)}, u32[]{:S(2)}) copy-start(s32[8,64]{1,0:T(8,128)} %param.7) | copy-start | bytes 6148
  19.3 53.3 %all-to-all-start = ((bf16[128,4,4096]{0,2,1:T(8,128)(2,1)}), bf16[128,4,4096]{0,2,1:T(8,128)(2,1)}, u32[]{:S(2)}, u32[]{:S(2)}) async-start(bf16[128,4,4096]{0,2,1:T(8,128)(2,1)} %bitcast.21), calls=%async_computation | async-start | bytes 8388608 | tf_op jit(solution)/shard_map/all_to_all | solution.py:15
  24.3 99.7 %reduce-scatter.2.cloned.1.call-start = ((), (), s32[]{:S(2)}) async-start(), calls=%async_computation.4 | async-start | bytes 1310720 | tf_op jit(solution)/shard_map/reduce_scatter | solution.py:26
  92.1 3.4 %copy-start = (bf16[512,4096]{1,0:T(8,128)(2,1)S(1)}, bf16[512,4096]{1,0:T(8,128)(2,1)}, u32[]{:S(2)}) copy-start(bf16[512,4096]{1,0:T(8,128)(2,1)} %bitcast_multiply_fusion) | copy-start | bytes 12582916
Sparse Core Ops, SparseCore 0:
  9.5 76.0 all-gather.1
  99.1 24.8 reduce-scatter.1
where the time goes:
time: 133 us; the launch traced here: 132 us
  waiting for transfers between devices  64 us (48%)
  local copies, waits for them, and re-layouts  31.6 us (24%)
  between operations  13.5 us (10%)
  other arithmetic  10.8 us (8%)
  starting transfers between devices  9.22 us (7%)
  matrix products  3.35 us (3%)
    all_to_all x1, waiting for transfers between devices, local(): lax.all_to_all(amplitudes, 'col', split_axis=1, concat_axis=0, tiled=True)  37.5 us
    reduce_scatter x1, waiting for transfers between devices, local(): lax.psum_scatter(partial_sums, 'col', scatter_dimension=0, tiled=True)  25 us
    unnamed x7, local copies, waits for them, and re-layouts  7.94 us
    convert_element_type x5, local copies, waits for them, and re-layouts, expand_mask(): jnp.repeat(jnp.repeat(tiles, TILE, axis=0), TILE, axis=1)  6.89 us
    all_gather x1, local copies, waits for them, and re-layouts, local(): lax.all_gather(integrals, 'row', axis=0, tiled=True) * panel_mask  6.49 us
    all_to_all x1, local copies, waits for them, and re-layouts, local(): lax.all_to_all(amplitudes, 'col', split_axis=1, concat_axis=0, tiled=True)  6.43 us
    mul x1, other arithmetic, local(): stored_amps = regrouped * expand_mask(regrouped_tiles)  5.85 us
    all_to_all x1, starting transfers between devices, local(): lax.all_to_all(amplitudes, 'col', split_axis=1, concat_axis=0, tiled=True)  4.97 us
  transfers between devices with their start and end apart: 4, of which 3 were waited for; matrix products, arithmetic and copies ran while one was open for 23% of the time, Pallas kernels for 0%

commit v1 on v0

v1 whole, which is shorter than its diff:
```python
import functools

import jax
import jax.numpy as jnp
from jax import lax
from jax.experimental import pallas as pl
from jax.experimental.pallas import tpu as pltpu
from jax.sharding import PartitionSpec as P

TILE = 64
LANES = 128
CHUNKS = 4
MESH = pl.DeviceIdType.MESH


def kernel(
    n_row, n_col, amp_ref, amp_tiles, int_ref, int_tiles, out_ref,
    raw, amps, ints_raw, ints, part, pair_in, chip_in,
    load_sem, int_load_sem, amp_send, amp_recv, ring_send, ring_recv, pair_send, pair_recv, chip_send, chip_recv,
):
    row, col = lax.axis_index("row"), lax.axis_index("col")
    n_chip = n_col // 2
    chip, core = col // 2, lax.rem(col, 2)
    n_pairs = amp_ref.shape[0]
    own_rows, depth = int_ref.shape
    width = depth // CHUNKS
    n_res = ints.shape[0]
    out_rows = n_res // n_col
    half = depth // 2

    def peer(chip_step, core_step):
        return lax.rem(chip + chip_step, n_chip) * 2 + lax.rem(core + core_step, 2)

    def at_position(position):
        position = lax.rem(position + n_row, n_row)
        return jnp.where(position < n_row // 2, 2 * position, 2 * (n_row - 1 - position) + 1)

    position = jnp.where(lax.rem(row, 2) == 0, row // 2, n_row - 1 - row // 2)
    right, left = at_position(position + 1), at_position(position - 1)

    order = [(chip_step, core_step) for chip_step in range(1, n_chip) for core_step in range(2)] + [(0, 1), (0, 0)]

    def slot_of(chip_step, core_step, chunk):
        return (chip_step * 2 + core_step) * CHUNKS + chunk

    int_load = pltpu.make_async_copy(int_ref, ints_raw, int_load_sem)
    int_load.start()
    loads = {}
    for chip_step, core_step in order:
        target = peer(chip_step, core_step)
        for chunk in range(CHUNKS):
            slot = slot_of(chip_step, core_step, chunk)
            start = pl.multiple_of(target * depth + chunk * width, LANES)
            loads[slot] = pltpu.make_async_copy(amp_ref.at[:, pl.ds(start, width)], raw.at[slot], load_sem.at[slot])
            loads[slot].start()

    barrier = pltpu.get_barrier_semaphore()
    for neighbour in (left, right):
        pl.semaphore_signal(barrier, inc=1, device_id={"row": neighbour}, device_id_type=MESH)
    for chip_step, core_step in order[:-1]:
        pl.semaphore_signal(barrier, inc=1, device_id={"col": peer(chip_step, core_step)}, device_id_type=MESH)

    first_half = lax.broadcasted_iota(jnp.int32, (16, LANES), 1) < TILE

    int_load.wait()
    own_start = pl.multiple_of(row * own_rows, 16)

    def mask_ints(block, _):
        lanes = pl.ds(pl.multiple_of(block * LANES, LANES), LANES)
        for group in range(own_rows // 16):
            tile_row = (own_start + group * 16) // TILE
            mask = jnp.where(first_half, int_tiles[tile_row, 2 * block], int_tiles[tile_row, 2 * block + 1])
            mask = mask.astype(jnp.float32).astype(jnp.bfloat16)
            ints[pl.ds(own_start + group * 16, 16), lanes] = ints_raw[pl.ds(group * 16, 16), lanes] * mask
        return 0

    lax.fori_loop(0, depth // LANES, mask_ints, 0)

    pl.semaphore_wait(barrier, 2 + n_col - 1)

    limits = ((n_row // 2, n_row - 1 - n_row // 2), (n_row - 1 - n_row // 2, n_row // 2))

    def ring_copy(direction, step, part_index):
        sign = 1 if direction == 0 else -1
        origin = at_position(position - sign * (step - 1))
        block = ints.at[pl.ds(pl.multiple_of(origin * own_rows, 16), own_rows), pl.ds(part_index * half, half)]
        return pltpu.make_async_remote_copy(
            src_ref=block, dst_ref=block,
            send_sem=ring_send.at[direction, step - 1, part_index],
            recv_sem=ring_recv.at[direction, step - 1, part_index],
            device_id={"row": right if direction == 0 else left}, device_id_type=MESH,
        )

    def ring_moves(step):
        return [(d, h) for h in range(2) for d in range(2) if step <= limits[d][h]]

    for direction, part_index in ring_moves(1):
        ring_copy(direction, 1, part_index).start()

    def masked_amps(slot, target, chunk, write):
        for tile_row in range(n_pairs // TILE):
            for block in range(width // LANES):
                tile = target * (depth // TILE) + chunk * (width // TILE) + 2 * block
                mask = jnp.where(first_half, amp_tiles[tile_row, tile], amp_tiles[tile_row, tile + 1])
                mask = mask.astype(jnp.float32).astype(jnp.bfloat16)
                for group in range(TILE // 16):
                    rows = pl.ds(tile_row * TILE + group * 16, 16)
                    write(tile_row * TILE + group * 16, block, raw[slot, rows, pl.ds(block * LANES, LANES)] * mask)

    def amp_copy(chip_step, core_step, chunk):
        slot = slot_of(chip_step, core_step, chunk)
        return pltpu.make_async_remote_copy(
            src_ref=raw.at[slot],
            dst_ref=amps.at[pl.ds(pl.multiple_of(col * n_pairs, 16), n_pairs), pl.ds(chunk * width, width)],
            send_sem=amp_send.at[slot], recv_sem=amp_recv.at[slot],
            device_id={"col": peer(chip_step, core_step)}, device_id_type=MESH,
        )

    sends = [(s, c, q) for q in range(CHUNKS) for s, c in order[:-2]] + [(0, 1, q) for q in range(CHUNKS)]
    for chip_step, core_step, chunk in sends:
        slot = slot_of(chip_step, core_step, chunk)
        loads[slot].wait()

        def write(row_start, block, value):
            raw[slot, pl.ds(row_start, 16), pl.ds(block * LANES, LANES)] = value

        masked_amps(slot, peer(chip_step, core_step), chunk, write)
        amp_copy(chip_step, core_step, chunk).start()
    own_pairs = pl.multiple_of(col * n_pairs, 16)
    for chunk in range(CHUNKS):
        slot = slot_of(0, 0, chunk)
        loads[slot].wait()

        def write(row_start, block, value):
            amps[pl.ds(own_pairs + row_start, 16), pl.ds(chunk * width + block * LANES, LANES)] = value

        masked_amps(slot, col, chunk, write)

    for step in range(1, n_row // 2 + 1):
        for direction, part_index in ring_moves(step):
            ring_copy(direction, step, part_index).wait_recv()
            if step + 1 <= limits[direction][part_index]:
                ring_copy(direction, step + 1, part_index).start()

    m_tile = 256

    def multiply(chip_step, chunk, first):
        source = lax.rem(chip - chip_step + n_chip, n_chip)
        pairs = pl.ds(pl.multiple_of(source * (2 * n_pairs), LANES), 2 * n_pairs)
        lanes = pl.ds(chunk * width, width)

        def body(tile, _):
            rows = pl.ds(pl.multiple_of(tile * m_tile, m_tile), m_tile)
            product = lax.dot_general(
                ints[rows, lanes], amps[pairs, lanes], (((1,), (1,)), ((), ())), preferred_element_type=jnp.float32
            )
            part[rows, pairs] = product if first else part[rows, pairs] + product
            return 0

        lax.fori_loop(0, n_res // m_tile, body, 0)

    for chunk in range(CHUNKS):
        amp_copy(0, 1, chunk).wait_recv()
        multiply(0, chunk, chunk == 0)
    for chunk in range(CHUNKS):
        for chip_step in range(1, n_chip):
            for core_step in range(2):
                amp_copy(chip_step, core_step, chunk).wait_recv()
            multiply(chip_step, chunk, chunk == 0)

    def res_rows(chip_step, core_step):
        return pl.ds(pl.multiple_of(peer(chip_step, core_step) * out_rows, 8), out_rows)

    def pair_copy(chip_step):
        return pltpu.make_async_remote_copy(
            src_ref=part.at[res_rows(chip_step, 1)], dst_ref=pair_in.at[chip_step],
            send_sem=pair_send.at[chip_step], recv_sem=pair_recv.at[chip_step],
            device_id={"col": peer(0, 1)}, device_id_type=MESH,
        )

    def chip_copy(chip_step):
        return pltpu.make_async_remote_copy(
            src_ref=part.at[res_rows(chip_step, 0)], dst_ref=chip_in.at[chip_step - 1],
            send_sem=chip_send.at[chip_step - 1], recv_sem=chip_recv.at[chip_step - 1],
            device_id={"col": peer(chip_step, 0)}, device_id_type=MESH,
        )

    steps = list(range(1, n_chip)) + [0]
    for chip_step in steps:
        pair_copy(chip_step).start()
    for chip_step in steps:
        pair_copy(chip_step).wait_recv()
        rows = res_rows(chip_step, 0)
        part[rows, :] = part[rows, :] + pair_in[chip_step]
        if chip_step:
            chip_copy(chip_step).start()
    total = part[res_rows(0, 0), :]
    for chip_step in range(1, n_chip):
        chip_copy(chip_step).wait_recv()
        total = total + chip_in[chip_step - 1]
    out_ref[...] = total.astype(out_ref.dtype)

    for chip_step, core_step, chunk in sends:
        amp_copy(chip_step, core_step, chunk).wait_send()
    for step in range(1, n_row // 2 + 1):
        for direction, part_index in ring_moves(step):
            ring_copy(direction, step, part_index).wait_send()
    for chip_step in steps:
        pair_copy(chip_step).wait_send()
        if chip_step:
            chip_copy(chip_step).wait_send()


def local(n_row, n_col, amplitudes, amp_tiles, integrals, int_tiles):
    n_pairs = amplitudes.shape[0]
    own_rows, depth = integrals.shape
    n_res, row_pairs = own_rows * n_row, n_pairs * n_col
    out_rows, n_chip = n_res // n_col, n_col // 2
    slots = n_col * CHUNKS
    return pl.pallas_call(
        functools.partial(kernel, n_row, n_col),
        out_shape=jax.ShapeDtypeStruct((out_rows, row_pairs), jnp.bfloat16),
        in_specs=[
            pl.BlockSpec(memory_space=pl.ANY),
            pl.BlockSpec(memory_space=pltpu.SMEM),
            pl.BlockSpec(memory_space=pl.ANY),
            pl.BlockSpec(memory_space=pltpu.SMEM),
        ],
        out_specs=pl.BlockSpec(memory_space=pltpu.VMEM),
        scratch_shapes=[
            pltpu.VMEM((slots, n_pairs, depth // CHUNKS), jnp.bfloat16),
            pltpu.VMEM((row_pairs, depth), jnp.bfloat16),
            pltpu.VMEM((own_rows, depth), jnp.bfloat16),
            pltpu.VMEM((n_res, depth), jnp.bfloat16),
            pltpu.VMEM((n_res, row_pairs), jnp.float32),
            pltpu.VMEM((n_chip, out_rows, row_pairs), jnp.float32),
            pltpu.VMEM((n_chip - 1, out_rows, row_pairs), jnp.float32),
            pltpu.SemaphoreType.DMA((slots,)),
            pltpu.SemaphoreType.DMA,
            pltpu.SemaphoreType.DMA((slots,)),
            pltpu.SemaphoreType.DMA((slots,)),
            pltpu.SemaphoreType.DMA((2, n_row // 2, 2)),
            pltpu.SemaphoreType.DMA((2, n_row // 2, 2)),
            pltpu.SemaphoreType.DMA((n_chip,)),
            pltpu.SemaphoreType.DMA((n_chip,)),
            pltpu.SemaphoreType.DMA((n_chip - 1,)),
            pltpu.SemaphoreType.DMA((n_chip - 1,)),
        ],
        compiler_params=pltpu.CompilerParams(
            collective_id=0, has_side_effects=True, vmem_limit_bytes=48 * 1024 * 1024
        ),
    )(amplitudes, amp_tiles, integrals, int_tiles)


def solution(mesh):
    return jax.shard_map(
        functools.partial(local, mesh.shape["row"], mesh.shape["col"]),
        mesh=mesh,
        in_specs=(
            P(("row", "col"), None),
            P(("row", "col"), None),
            P("row", "col"),
            P(None, "col"),
        ),
        out_specs=P("col", "row"),
        check_vma=False,
    )
```

time: 133 us -> 66.7 us (0.50)
  waiting for transfers between devices: 64 us -> 0 us
  Pallas kernels: 0 us -> 61 us
  local copies, waits for them, and re-layouts: 31.6 us -> 5.25 us
  between operations: 13.5 us -> 0.01 us
  other arithmetic: 10.8 us -> 0 us
  starting transfers between devices: 9.22 us -> 0 us
  matrix products: 3.35 us -> 0 us
    pallas_call x0 -> x1, Pallas kernels: none -> 61 us  [local(): pl.pallas_call(functools.partial(kernel, n_row, n_col), out_shape=jax.Sha...]
    all_to_all x2 -> x0, waiting for transfers between devices: 37.5 us -> none  [the longest x1 37.5 us: local(): lax.all_to_all(amplitudes, 'col', split_axis=1, concat_axis=0, tiled=True)]
    reduce_scatter x1 -> x0, waiting for transfers between devices: 25 us -> none  [local(): lax.psum_scatter(partial_sums, 'col', scatter_dimension=0, tiled=True)]
    all_to_all x2 -> x0, starting transfers between devices: 9.18 us -> none  [the longest x1 4.97 us: local(): lax.all_to_all(amplitudes, 'col', split_axis=1, concat_axis=0, tiled=True)]
    mul x2 -> x0, other arithmetic: 8.49 us -> none  [the longest x1 5.85 us: local(): stored_amps = regrouped * expand_mask(regrouped_tiles)]
    all_to_all x4 -> x0, local copies, waits for them, and re-layouts: 7.72 us -> none  [the longest x1 6.43 us: local(): lax.all_to_all(amplitudes, 'col', split_axis=1, concat_axis=0, tiled=True)]
    convert_element_type x5 -> x0, local copies, waits for them, and re-layouts: 6.89 us -> none  [expand_mask(): jnp.repeat(jnp.repeat(tiles, TILE, axis=0), TILE, axis=1)]
    all_gather x1 -> x0, local copies, waits for them, and re-layouts: 6.49 us -> none  [local(): lax.all_gather(integrals, 'row', axis=0, tiled=True) * panel_mask]
  transfers between devices with their start and end apart: 4 -> 0, of which waited for: 3 -> 0; matrix products, arithmetic and copies ran while one was open for 23% -> 0% of each run, Pallas kernels for 0% -> 0%
where the time goes in v1:
time: 66.7 us; the launch traced here: 66.3 us
  Pallas kernels  61 us (91%)
  local copies, waits for them, and re-layouts  5.25 us (8%)
    pallas_call x1, Pallas kernels, local(): pl.pallas_call(functools.partial(kernel, n_row, n_col), out_shape=jax.Sha...  61 us
    unnamed x9, local copies, waits for them, and re-layouts  5.25 us

profile of v1, /device:TPU:0, one launch (start us, length us, event | category | flops | bytes accessed | tf_op | source)
XLA Modules:
  0.0 66.3 jit_solution(14121521580441399282)
XLA Ops:
  0.0 0.0 copy-start
  0.0 2.2 %copy-done = bf16[128,16384]{1,0:T(8,128)(2,1)S(1)} copy-done((bf16[128,16384]{1,0:T(8,128)(2,1)S(1)}, bf16[128,16384]{1,0:T(8,128)(2,1)}, u32[]{:S(2)}) %copy-start) | copy-done | bytes 4194328
  2.2 0.0 copy-start.1
  2.2 1.0 %copy-done.1 = bf16[64,4096]{1,0:T(8,128)(2,1)S(1)} copy-done((bf16[64,4096]{1,0:T(8,128)(2,1)S(1)}, bf16[64,4096]{1,0:T(8,128)(2,1)}, u32[]{:S(2)}) %copy-start.1) | copy-done | bytes 524312
  3.2 0.0 copy-start.2
  3.2 0.7 %copy-done.2 = s32[8,64]{1,0:T(8,128)S(1)} copy-done((s32[8,64]{1,0:T(8,128)S(1)}, s32[8,64]{1,0:T(8,128)}, u32[]{:S(2)}) %copy-start.2) | copy-done | bytes 2072
  3.9 0.0 copy-start.3
  3.9 0.7 %copy-done.3 = s32[2,256]{1,0:T(2,128)S(1)} copy-done((s32[2,256]{1,0:T(2,128)S(1)}, s32[2,256]{1,0:T(2,128)}, u32[]{:S(2)}) %copy-start.3) | copy-done | bytes 2072
  4.6 61.0 %shard_map.46 = bf16[128,512]{1,0:T(8,128)(2,1)S(1)} custom-call(bf16[128,16384]{1,0:T(8,128)(2,1)S(1)} %copy-done, s32[2,256]{1,0:T(2,128)S(1)} %copy-done.3, bf16[64,4096]{1,0:T(8,128)(2,1)S(1)} %copy-done.1, s32[8,64]{1,0:T(8,128)S(1)} %copy-done.2), custom_call_target="tpu_custom_call" | custom-call | tf_op jit(solution)/shard_map/pallas_call | solution.py:220
  65.6 0.7 copy.6
Async XLA Ops:
  0.0 2.2 %copy-start = (bf16[128,16384]{1,0:T(8,128)(2,1)S(1)}, bf16[128,16384]{1,0:T(8,128)(2,1)}, u32[]{:S(2)}) copy-start(bf16[128,16384]{1,0:T(8,128)(2,1)} %amp_ref.1) | copy-start | bytes 12582916
  2.2 1.0 %copy-start.1 = (bf16[64,4096]{1,0:T(8,128)(2,1)S(1)}, bf16[64,4096]{1,0:T(8,128)(2,1)}, u32[]{:S(2)}) copy-start(bf16[64,4096]{1,0:T(8,128)(2,1)} %int_ref.1) | copy-start | bytes 1572868
  3.2 0.7 %copy-start.2 = (s32[8,64]{1,0:T(8,128)S(1)}, s32[8,64]{1,0:T(8,128)}, u32[]{:S(2)}) copy-start(s32[8,64]{1,0:T(8,128)} %int_tiles.1) | copy-start | bytes 6148
  3.9 0.7 %copy-start.3 = (s32[2,256]{1,0:T(2,128)S(1)}, s32[2,256]{1,0:T(2,128)}, u32[]{:S(2)}) copy-start(s32[2,256]{1,0:T(2,128)} %amp_tiles.1) | copy-start | bytes 6148

commit v2 on v1

v2 whole, which is shorter than its diff:
```python
import functools

import jax
import jax.numpy as jnp
from jax import lax
from jax.experimental import pallas as pl
from jax.experimental.pallas import tpu as pltpu
from jax.sharding import PartitionSpec as P

TILE = 64
LANES = 128
CHUNKS = 4
MESH = pl.DeviceIdType.MESH


def kernel(
    n_row, n_col, amp_ref, amp_tiles_ref, int_ref, int_tiles_ref, out_ref,
    amp_tiles, int_tiles, tile_sem, raw, amps, ints_raw, ints, part, pair_in, chip_in,
    load_sem, int_load_sem, amp_send, amp_recv, ring_send, ring_recv, pair_send, pair_recv, chip_send, chip_recv,
):
    row, col = lax.axis_index("row"), lax.axis_index("col")
    n_chip = n_col // 2
    chip, core = col // 2, lax.rem(col, 2)
    n_pairs = amp_ref.shape[0]
    own_rows, depth = int_ref.shape
    width = depth // CHUNKS
    n_res = ints.shape[0]
    out_rows = n_res // n_col
    half = depth // 2

    def peer(chip_step, core_step):
        return lax.rem(chip + chip_step, n_chip) * 2 + lax.rem(core + core_step, 2)

    def at_position(position):
        position = lax.rem(position + n_row, n_row)
        return jnp.where(position < n_row // 2, 2 * position, 2 * (n_row - 1 - position) + 1)

    position = jnp.where(lax.rem(row, 2) == 0, row // 2, n_row - 1 - row // 2)
    right, left = at_position(position + 1), at_position(position - 1)

    order = [(chip_step, core_step) for chip_step in range(1, n_chip) for core_step in range(2)] + [(0, 1), (0, 0)]

    barrier = pltpu.get_barrier_semaphore()
    for neighbour in (left, right):
        pl.semaphore_signal(barrier, inc=1, device_id={"row": neighbour}, device_id_type=MESH)
    for chip_step, core_step in order[:-1]:
        pl.semaphore_signal(barrier, inc=1, device_id={"col": peer(chip_step, core_step)}, device_id_type=MESH)

    def slot_of(chip_step, core_step, chunk):
        return (chip_step * 2 + core_step) * CHUNKS + chunk

    sends = [(s, c, q) for q in range(CHUNKS) for s, c in order[:-2]] + [(0, 1, q) for q in range(CHUNKS)]

    int_load = pltpu.make_async_copy(int_ref, ints_raw, int_load_sem)
    tile_loads = [
        pltpu.make_async_copy(amp_tiles_ref, amp_tiles, tile_sem.at[0]),
        pltpu.make_async_copy(int_tiles_ref, int_tiles, tile_sem.at[1]),
    ]
    for load in tile_loads:
        load.start()
    loads = {}
    for chip_step, core_step in order:
        target = peer(chip_step, core_step)
        for chunk in range(CHUNKS):
            slot = slot_of(chip_step, core_step, chunk)
            start = pl.multiple_of(target * depth + chunk * width, LANES)
            loads[slot] = pltpu.make_async_copy(amp_ref.at[:, pl.ds(start, width)], raw.at[slot], load_sem.at[slot])
    for index, (chip_step, core_step, chunk) in enumerate(sends + [(0, 0, q) for q in range(CHUNKS)]):
        loads[slot_of(chip_step, core_step, chunk)].start()
        if index == 0:
            int_load.start()

    first_half = lax.broadcasted_iota(jnp.int32, (16, LANES), 1) < TILE

    def masked_amps(slot, target, chunk, write):
        for tile_row in range(n_pairs // TILE):
            for block in range(width // LANES):
                tile = target * (depth // TILE) + chunk * (width // TILE) + 2 * block
                mask = jnp.where(first_half, amp_tiles[tile_row, tile], amp_tiles[tile_row, tile + 1])
                mask = mask.astype(jnp.float32).astype(jnp.bfloat16)
                for group in range(TILE // 16):
                    rows = pl.ds(tile_row * TILE + group * 16, 16)
                    write(tile_row * TILE + group * 16, block, raw[slot, rows, pl.ds(block * LANES, LANES)] * mask)

    def amp_copy(chip_step, core_step, chunk):
        slot = slot_of(chip_step, core_step, chunk)
        return pltpu.make_async_remote_copy(
            src_ref=raw.at[slot],
            dst_ref=amps.at[pl.ds(pl.multiple_of(col * n_pairs, 16), n_pairs), pl.ds(chunk * width, width)],
            send_sem=amp_send.at[slot], recv_sem=amp_recv.at[slot],
            device_id={"col": peer(chip_step, core_step)}, device_id_type=MESH,
        )

    def prepare_amps(chip_step, core_step, chunk):
        slot = slot_of(chip_step, core_step, chunk)
        loads[slot].wait()

        def write(row_start, block, value):
            raw[slot, pl.ds(row_start, 16), pl.ds(block * LANES, LANES)] = value

        masked_amps(slot, peer(chip_step, core_step), chunk, write)
    tile_loads[0].wait()
    prepare_amps(*sends[0])
    pl.semaphore_wait(barrier, 2 + n_col - 1)
    amp_copy(*sends[0]).start()

    int_load.wait()
    tile_loads[1].wait()
    own_start = pl.multiple_of(row * own_rows, 16)

    def mask_ints(block, _):
        lanes = pl.ds(pl.multiple_of(block * LANES, LANES), LANES)
        for group in range(own_rows // 16):
            tile_row = (own_start + group * 16) // TILE
            mask = jnp.where(first_half, int_tiles[tile_row, 2 * block], int_tiles[tile_row, 2 * block + 1])
            mask = mask.astype(jnp.float32).astype(jnp.bfloat16)
            ints[pl.ds(own_start + group * 16, 16), lanes] = ints_raw[pl.ds(group * 16, 16), lanes] * mask
        return 0

    lax.fori_loop(0, depth // LANES, mask_ints, 0)

    limits = ((n_row // 2, n_row - 1 - n_row // 2), (n_row - 1 - n_row // 2, n_row // 2))

    def ring_copy(direction, step, part_index):
        sign = 1 if direction == 0 else -1
        origin = at_position(position - sign * (step - 1))
        block = ints.at[pl.ds(pl.multiple_of(origin * own_rows, 16), own_rows), pl.ds(part_index * half, half)]
        return pltpu.make_async_remote_copy(
            src_ref=block, dst_ref=block,
            send_sem=ring_send.at[direction, step - 1, part_index],
            recv_sem=ring_recv.at[direction, step - 1, part_index],
            device_id={"row": right if direction == 0 else left}, device_id_type=MESH,
        )

    def ring_moves(step):
        return [(d, h) for h in range(2) for d in range(2) if step <= limits[d][h]]

    for direction, part_index in ring_moves(1):
        ring_copy(direction, 1, part_index).start()

    for send in sends[1:]:
        prepare_amps(*send)
        amp_copy(*send).start()

    own_pairs = pl.multiple_of(col * n_pairs, 16)
    for chunk in range(CHUNKS):
        slot = slot_of(0, 0, chunk)
        loads[slot].wait()

        def write(row_start, block, value):
            amps[pl.ds(own_pairs + row_start, 16), pl.ds(chunk * width + block * LANES, LANES)] = value

        masked_amps(slot, col, chunk, write)

    for step in range(1, n_row // 2 + 1):
        for direction, part_index in ring_moves(step):
            ring_copy(direction, step, part_index).wait_recv()
            if step + 1 <= limits[direction][part_index]:
                ring_copy(direction, step + 1, part_index).start()

    m_tile = 256

    def multiply(chip_step, chunk, first):
        pairs = group_pairs(chip_step)
        lanes = pl.ds(chunk * width, width)

        def body(tile, _):
            rows = pl.ds(pl.multiple_of(tile * m_tile, m_tile), m_tile)
            product = lax.dot_general(
                ints[rows, lanes], amps[pairs, lanes], (((1,), (1,)), ((), ())), preferred_element_type=jnp.float32
            )
            part[rows, pairs] = product if first else part[rows, pairs] + product
            return 0

        lax.fori_loop(0, n_res // m_tile, body, 0)

    def res_rows(chip_step, core_step):
        return pl.ds(pl.multiple_of(peer(chip_step, core_step) * out_rows, 8), out_rows)

    def group_pairs(group):
        source = lax.rem(chip - group + n_chip, n_chip)
        return pl.ds(pl.multiple_of(source * (2 * n_pairs), LANES), 2 * n_pairs)

    def pair_copy(group, chip_step):
        pairs = group_pairs(group)
        return pltpu.make_async_remote_copy(
            src_ref=part.at[res_rows(chip_step, 1), pairs], dst_ref=pair_in.at[chip_step, :, pairs],
            send_sem=pair_send.at[group, chip_step], recv_sem=pair_recv.at[group, chip_step],
            device_id={"col": peer(0, 1)}, device_id_type=MESH,
        )

    def chip_copy(group, chip_step):
        pairs = group_pairs(group)
        return pltpu.make_async_remote_copy(
            src_ref=part.at[res_rows(chip_step, 0), pairs], dst_ref=chip_in.at[chip_step - 1, :, pairs],
            send_sem=chip_send.at[group, chip_step - 1], recv_sem=chip_recv.at[group, chip_step - 1],
            device_id={"col": peer(chip_step, 0)}, device_id_type=MESH,
        )

    def chip_arrival(group, chip_step):
        pairs = group_pairs(group)
        sender_group = (group - chip_step) % n_chip
        return pltpu.make_async_remote_copy(
            src_ref=part.at[res_rows(chip_step, 0), pairs], dst_ref=chip_in.at[chip_step - 1, :, pairs],
            send_sem=chip_send.at[sender_group, chip_step - 1], recv_sem=chip_recv.at[sender_group, chip_step - 1],
            device_id={"col": peer(chip_step, 0)}, device_id_type=MESH,
        )

    steps = list(range(1, n_chip)) + [0]

    def exchange(group):
        for chip_step in steps:
            pair_copy(group, chip_step).start()

    def pass_on(group):
        pairs = group_pairs(group)
        for chip_step in steps:
            pair_copy(group, chip_step).wait_recv()
            rows = res_rows(chip_step, 0)
            part[rows, pairs] = part[rows, pairs] + pair_in[chip_step, :, pairs]
            if chip_step:
                chip_copy(group, chip_step).start()

    for chunk in range(CHUNKS):
        amp_copy(0, 1, chunk).wait_recv()
        multiply(0, chunk, chunk == 0)
    exchange(0)
    for group in range(1, n_chip):
        for chunk in range(CHUNKS):
            for core_step in range(2):
                amp_copy(group, core_step, chunk).wait_recv()
            multiply(group, chunk, chunk == 0)
            if group == 1 and chunk == 0:
                pass_on(0)
        exchange(group)
    for group in range(1, n_chip):
        pass_on(group)
    for group in range(n_chip):
        pairs = group_pairs(group)
        total = part[res_rows(0, 0), pairs]
        for chip_step in range(1, n_chip):
            chip_arrival(group, chip_step).wait_recv()
            total = total + chip_in[chip_step - 1, :, pairs]
        out_ref[:, pairs] = total.astype(out_ref.dtype)

    for chip_step, core_step, chunk in sends:
        amp_copy(chip_step, core_step, chunk).wait_send()
    for step in range(1, n_row // 2 + 1):
        for direction, part_index in ring_moves(step):
            ring_copy(direction, step, part_index).wait_send()
    for group in range(n_chip):
        for chip_step in steps:
            pair_copy(group, chip_step).wait_send()
            if chip_step:
                chip_copy(group, chip_step).wait_send()


def local(n_row, n_col, amplitudes, amp_tiles, integrals, int_tiles):
    n_pairs = amplitudes.shape[0]
    own_rows, depth = integrals.shape
    n_res, row_pairs = own_rows * n_row, n_pairs * n_col
    out_rows, n_chip = n_res // n_col, n_col // 2
    slots = n_col * CHUNKS
    return pl.pallas_call(
        functools.partial(kernel, n_row, n_col),
        out_shape=jax.ShapeDtypeStruct((out_rows, row_pairs), jnp.bfloat16),
        in_specs=[
            pl.BlockSpec(memory_space=pltpu.HBM),
            pl.BlockSpec(memory_space=pltpu.HBM),
            pl.BlockSpec(memory_space=pltpu.HBM),
            pl.BlockSpec(memory_space=pltpu.HBM),
        ],
        out_specs=pl.BlockSpec(memory_space=pltpu.VMEM),
        scratch_shapes=[
            pltpu.SMEM(amp_tiles.shape, jnp.int32),
            pltpu.SMEM(int_tiles.shape, jnp.int32),
            pltpu.SemaphoreType.DMA((2,)),
            pltpu.VMEM((slots, n_pairs, depth // CHUNKS), jnp.bfloat16),
            pltpu.VMEM((row_pairs, depth), jnp.bfloat16),
            pltpu.VMEM((own_rows, depth), jnp.bfloat16),
            pltpu.VMEM((n_res, depth), jnp.bfloat16),
            pltpu.VMEM((n_res, row_pairs), jnp.float32),
            pltpu.VMEM((n_chip, out_rows, row_pairs), jnp.float32),
            pltpu.VMEM((n_chip - 1, out_rows, row_pairs), jnp.float32),
            pltpu.SemaphoreType.DMA((slots,)),
            pltpu.SemaphoreType.DMA,
            pltpu.SemaphoreType.DMA((slots,)),
            pltpu.SemaphoreType.DMA((slots,)),
            pltpu.SemaphoreType.DMA((2, n_row // 2, 2)),
            pltpu.SemaphoreType.DMA((2, n_row // 2, 2)),
            pltpu.SemaphoreType.DMA((n_chip, n_chip)),
            pltpu.SemaphoreType.DMA((n_chip, n_chip)),
            pltpu.SemaphoreType.DMA((n_chip, n_chip - 1)),
            pltpu.SemaphoreType.DMA((n_chip, n_chip - 1)),
        ],
        compiler_params=pltpu.CompilerParams(
            collective_id=0, has_side_effects=True, vmem_limit_bytes=64 * 1024 * 1024
        ),
    )(amplitudes, amp_tiles, integrals, int_tiles)


def solution(mesh):
    return jax.shard_map(
        functools.partial(local, mesh.shape["row"], mesh.shape["col"]),
        mesh=mesh,
        in_specs=(
            P(("row", "col"), None),
            P(("row", "col"), None),
            P("row", "col"),
            P(None, "col"),
        ),
        out_specs=P("col", "row"),
        check_vma=False,
    )
```

time: 66.7 us -> 63.6 us (0.954)
  local copies, waits for them, and re-layouts: 5.25 us -> 1.57 us
  Pallas kernels: 61 us -> 61.9 us
    unnamed x9 -> x1, local copies, waits for them, and re-layouts: 5.25 us -> 1.57 us
    pallas_call x1, Pallas kernels: 61 us -> 61.9 us  [local(): pl.pallas_call(functools.partial(kernel, n_row, n_col), out_shape=jax.Sha...]
where the time goes in v2:
time: 63.6 us; the launch traced here: 63.5 us
  Pallas kernels  61.9 us (97%)
  local copies, waits for them, and re-layouts  1.57 us (2%)
    pallas_call x1, Pallas kernels, local(): pl.pallas_call(functools.partial(kernel, n_row, n_col), out_shape=jax.Sha...  61.9 us
    unnamed x1, local copies, waits for them, and re-layouts  1.57 us

profile of v2, /device:TPU:0, one launch (start us, length us, event | category | flops | bytes accessed | tf_op | source)
XLA Modules:
  0.0 63.5 jit_solution(16146050227576752143)
XLA Ops:
  0.0 61.9 %shard_map.46 = bf16[128,512]{1,0:T(8,128)(2,1)} custom-call(bf16[128,16384]{1,0:T(8,128)(2,1)} %amp_ref.1, s32[2,256]{1,0:T(2,128)} %amp_tiles_ref.1, bf16[64,4096]{1,0:T(8,128)(2,1)} %int_ref.1, s32[8,64]{1,0:T(8,128)} %int_tiles_ref.1), custom_call_target="tpu_custom_call" | custom-call | tf_op jit(solution)/shard_map/pallas_call | solution.py:264
  61.9 1.6 %copy.6 = bf16[128,512]{1,0:T(8,128)(2,1)} copy(bf16[128,512]{1,0:T(8,128)(2,1)} %shard_map.46) | data formatting | bytes 262144

commit v3 on v2

--- a/solution.py
+++ b/solution.py
@@ -9,7 +9,7 @@
 
 TILE = 64
 LANES = 128
-CHUNKS = 4
+CHUNKS = 2
 MESH = pl.DeviceIdType.MESH
 
 
@@ -49,7 +49,8 @@
     def slot_of(chip_step, core_step, chunk):
         return (chip_step * 2 + core_step) * CHUNKS + chunk
 
-    sends = [(s, c, q) for q in range(CHUNKS) for s, c in order[:-2]] + [(0, 1, q) for q in range(CHUNKS)]
+    across = [(s, c, q) for q in range(CHUNKS) for s, c in order[:-2]]
+    sends = across[:2] + [(0, 1, q) for q in range(CHUNKS)] + across[2:]
 
     int_load = pltpu.make_async_copy(int_ref, ints_raw, int_load_sem)
     tile_loads = [
@@ -161,7 +162,8 @@
     m_tile = 256
 
     def multiply(chip_step, chunk, first):
-        pairs = group_pairs(chip_step)
+        source = lax.rem(chip - chip_step + n_chip, n_chip)
+        pairs = pl.ds(pl.multiple_of(source * (2 * n_pairs), LANES), 2 * n_pairs)
         lanes = pl.ds(chunk * width, width)
 
         def body(tile, _):
@@ -178,8 +180,8 @@
         return pl.ds(pl.multiple_of(peer(chip_step, core_step) * out_rows, 8), out_rows)
 
     def group_pairs(group):
-        source = lax.rem(chip - group + n_chip, n_chip)
-        return pl.ds(pl.multiple_of(source * (2 * n_pairs), LANES), 2 * n_pairs)
+        source = lax.rem(chip - group // 2 + n_chip, n_chip)
+        return pl.ds(pl.multiple_of(source * (2 * n_pairs) + group % 2 * n_pairs, LANES), n_pairs)
 
     def pair_copy(group, chip_step):
         pairs = group_pairs(group)
@@ -199,7 +201,7 @@
 
     def chip_arrival(group, chip_step):
         pairs = group_pairs(group)
-        sender_group = (group - chip_step) % n_chip
+        sender_group = (group - 2 * chip_step) % n_col
         return pltpu.make_async_remote_copy(
             src_ref=part.at[res_rows(chip_step, 0), pairs], dst_ref=chip_in.at[chip_step - 1, :, pairs],
             send_sem=chip_send.at[sender_group, chip_step - 1], recv_sem=chip_recv.at[sender_group, chip_step - 1],
@@ -225,17 +227,20 @@
         amp_copy(0, 1, chunk).wait_recv()
         multiply(0, chunk, chunk == 0)
     exchange(0)
-    for group in range(1, n_chip):
+    exchange(1)
+    for chip_step in range(1, n_chip):
         for chunk in range(CHUNKS):
             for core_step in range(2):
-                amp_copy(group, core_step, chunk).wait_recv()
-            multiply(group, chunk, chunk == 0)
-            if group == 1 and chunk == 0:
+                amp_copy(chip_step, core_step, chunk).wait_recv()
+            multiply(chip_step, chunk, chunk == 0)
+            if chip_step == 1 and chunk == 0:
                 pass_on(0)
-        exchange(group)
-    for group in range(1, n_chip):
+                pass_on(1)
+        exchange(2 * chip_step)
+        exchange(2 * chip_step + 1)
+    for group in range(2, n_col):
         pass_on(group)
-    for group in range(n_chip):
+    for group in range(n_col):
         pairs = group_pairs(group)
         total = part[res_rows(0, 0), pairs]
         for chip_step in range(1, n_chip):
@@ -248,7 +253,7 @@
     for step in range(1, n_row // 2 + 1):
         for direction, part_index in ring_moves(step):
             ring_copy(direction, step, part_index).wait_send()
-    for group in range(n_chip):
+    for group in range(n_col):
         for chip_step in steps:
             pair_copy(group, chip_step).wait_send()
             if chip_step:
@@ -288,10 +293,10 @@
             pltpu.SemaphoreType.DMA((slots,)),
             pltpu.SemaphoreType.DMA((2, n_row // 2, 2)),
             pltpu.SemaphoreType.DMA((2, n_row // 2, 2)),
-            pltpu.SemaphoreType.DMA((n_chip, n_chip)),
-            pltpu.SemaphoreType.DMA((n_chip, n_chip)),
-            pltpu.SemaphoreType.DMA((n_chip, n_chip - 1)),
-            pltpu.SemaphoreType.DMA((n_chip, n_chip - 1)),
+            pltpu.SemaphoreType.DMA((n_col, n_chip)),
+            pltpu.SemaphoreType.DMA((n_col, n_chip)),
+            pltpu.SemaphoreType.DMA((n_col, n_chip - 1)),
+            pltpu.SemaphoreType.DMA((n_col, n_chip - 1)),
         ],
         compiler_params=pltpu.CompilerParams(
             collective_id=0, has_side_effects=True, vmem_limit_bytes=64 * 1024 * 1024

time: 63.6 us -> 62.5 us (0.983)
  Pallas kernels: 61.9 us -> 60.8 us
    pallas_call x1, Pallas kernels: 61.9 us -> 60.8 us  [local(): pl.pallas_call(functools.partial(kernel, n_row, n_col), out_shape=jax.Sha...]
where the time goes in v3:
time: 62.5 us; the launch traced here: 62.4 us
  Pallas kernels  60.8 us (97%)
  local copies, waits for them, and re-layouts  1.57 us (3%)
    pallas_call x1, Pallas kernels, local(): pl.pallas_call(functools.partial(kernel, n_row, n_col), out_shape=jax.Sha...  60.8 us
    unnamed x1, local copies, waits for them, and re-layouts  1.57 us

profile of v3, /device:TPU:0, one launch (start us, length us, event | category | flops | bytes accessed | tf_op | source)
XLA Modules:
  0.0 62.4 jit_solution(380912524067519449)
XLA Ops:
  0.0 60.8 %shard_map.46 = bf16[128,512]{1,0:T(8,128)(2,1)} custom-call(bf16[128,16384]{1,0:T(8,128)(2,1)} %amp_ref.1, s32[2,256]{1,0:T(2,128)} %amp_tiles_ref.1, bf16[64,4096]{1,0:T(8,128)(2,1)} %int_ref.1, s32[8,64]{1,0:T(8,128)} %int_tiles_ref.1), custom_call_target="tpu_custom_call" | custom-call | tf_op jit(solution)/shard_map/pallas_call | solution.py:269
  60.8 1.6 %copy.6 = bf16[128,512]{1,0:T(8,128)(2,1)} copy(bf16[128,512]{1,0:T(8,128)(2,1)} %shard_map.46) | data formatting | bytes 262144
